TPU v7x, 32 devices: a whole 2x2x4 slice. The times are simulated.
32 devices in a mesh: frame: 8 (over y, x, core), head: 4 (over z).
Axes of the slice: x: 2, y: 2, z: 4, core: 2. Of those that a mesh axis runs over, the one named last changes fastest.
Arguments:
- queries: bfloat16 [4096, 5120], P(('frame', 'head')), may hold values from -6 to 6, as said below
- keys: bfloat16 [4096, 5120], P(('frame', 'head')), may hold values from -6 to 6, as said below
- values: bfloat16 [4096, 5120], P(('frame', 'head')), may hold values from -6 to 6
- q_gain: float32 [5120], replicated, may hold values from 0.5 to 2
- k_gain: float32 [5120], replicated, may hold values from 0.5 to 2
- block_ids: int32 [8, 4, 8], P('frame'), may hold values from 0 to 11, as said below
- counts: int32 [8, 4], P('frame'), may hold values from 1 to 8, as said below
- anchors: int32 [2], replicated, may hold values from 0 to 7, as said below
Outputs:
- attended: bfloat16 [4096, 5120], P(('frame', 'head'))
Inputs may be any that keep to these rules, and one draw needn't show every extreme that they name: `queries`: away from rare tokens, entries are of order one. `keys`: away from rare tokens, entries are of order one. `block_ids`: the 8 entries of one list are different; the first is the query block's own block b. `counts`: every view has a query block that uses all 8 listed blocks. `anchors`: the 2 anchor ids are different; one of them is the last view, 7.
All inputs are finite; a program needn't handle non-finite values.
Results may differ from a plain program's by a relative error of at most 0.012.
The roundings to bfloat16 on the way count: a program that leaves them out, or rounds other values in their place, can miss the bound.
Values may be sent and summed in bfloat16 or wider, within the bound.
A program may use at most 128 MiB of HBM per device.

v0:
```python
import math

import jax
import jax.numpy as jnp
from jax import lax
from jax.sharding import PartitionSpec as P

HD = 128
BLOCK = 128


def spread(block, axis, owner):
    block = jnp.where(lax.axis_index(axis) == owner, block, jnp.zeros_like(block))
    return lax.psum(block, axis)


def normalize(rows, gain):
    wide = rows.astype(jnp.float32)
    square = jnp.mean(wide * wide, axis=-1, keepdims=True)
    return (wide * lax.rsqrt(square + 1e-06) * gain).astype(jnp.bfloat16)


def attend_view(q_heads, k_heads, v_heads, far_keys, far_values, block_ids, counts):
    view_len, local_width = q_heads.shape
    local_heads = local_width // HD
    blocks = view_len // BLOCK
    listed = block_ids.shape[2]
    group = math.gcd(blocks, max(1, 512 // BLOCK))
    steps = blocks // group
    key_blocks = jnp.concatenate([k_heads] + far_keys, axis=0).reshape(-1, BLOCK, local_heads, HD)
    value_blocks = jnp.concatenate([v_heads] + far_values, axis=0).reshape(
        -1, BLOCK, local_heads, HD
    )
    query_groups = q_heads.reshape(steps, group, BLOCK, local_heads, HD)
    id_groups = block_ids[0].reshape(steps, group, listed)
    count_groups = counts[0].reshape(steps, group)
    scale = 1.0 / math.sqrt(HD)
    slots = jnp.arange(listed, dtype=jnp.int32)

    def one_group(args):
        query_rows, id_lists, amount = args
        picked_k = key_blocks[id_lists]
        picked_v = value_blocks[id_lists]
        scores = (
            jnp.einsum(
                "gqhd,gkphd->ghqkp", query_rows, picked_k, preferred_element_type=jnp.float32
            )
            * scale
        )
        valid = (slots[None, :] < amount[:, None])[:, None, None, :, None]
        scores = jnp.where(valid, scores, -1e30)
        top = jnp.max(scores, axis=(3, 4), keepdims=True)
        expo = jnp.exp(scores - top)
        weights = (expo / jnp.sum(expo, axis=(3, 4), keepdims=True)).astype(jnp.bfloat16)
        mixed = jnp.einsum(
            "ghqkp,gkphd->gqhd", weights, picked_v, preferred_element_type=jnp.float32
        )
        return mixed.astype(jnp.bfloat16)

    result = lax.map(one_group, (query_groups, id_groups, count_groups))
    return result.reshape(view_len, local_width)


def shards(queries, keys, values, q_gain, k_gain, block_ids, counts, anchors):
    q_norm = normalize(queries, q_gain)
    k_norm = normalize(keys, k_gain)
    anchor_total = anchors.shape[0]
    far_keys = []
    far_values = []
    q_heads, k_heads, v_heads = (
        lax.all_to_all(q_norm, "head", split_axis=1, concat_axis=0, tiled=True),
        lax.all_to_all(k_norm, "head", split_axis=1, concat_axis=0, tiled=True),
        lax.all_to_all(values, "head", split_axis=1, concat_axis=0, tiled=True),
    )
    for anchor_slot in range(anchor_total):
        arrived = spread(jnp.stack([k_heads, v_heads]), "frame", anchors[anchor_slot])
        far_keys.append(arrived[0])
        far_values.append(arrived[1])
    mixed = attend_view(q_heads, k_heads, v_heads, far_keys, far_values, block_ids, counts)
    return lax.all_to_all(mixed, "head", split_axis=0, concat_axis=1, tiled=True)


def solution(mesh):
    placed = (
        P(("frame", "head"), None),
        P(("frame", "head"), None),
        P(("frame", "head"), None),
        P(),
        P(),
        P("frame", None, None),
        P("frame", None),
        P(),
    )
    return jax.shard_map(
        shards, mesh=mesh, in_specs=placed, out_specs=P(("frame", "head"), None), check_vma=False
    )
```

profile of v0, /device:TPU:0, one launch (start us, length us, event | category | flops | bytes accessed | tf_op | source)
XLA Modules:
  0.0 319.8 jit_solution(9023033393631996533)
XLA Ops:
  6.5 1.8 copy.23
  8.3 0.0 copy-start.2
  8.3 0.7 fusion.5
  9.0 0.0 copy-done.3
  9.0 3.0 fusion.7
  12.1 6.4 %all-to-all-start.1 = ((bf16[128,4,1280]{0,2,1:T(8,128)(2,1)}), bf16[128,4,1280]{0,2,1:T(8,128)(2,1)S(1)}, u32[]{:S(2)}, u32[]{:S(2)}) async-start(bf16[128,4,1280]{0,2,1:T(8,128)(2,1)} %bitcast.4), calls=%async_computation.1 | async-start | bytes 2621440 | tf_op jit(solution)/shard_map/all_to_all | solution.py:72
  18.5 0.0 copy-done.2
  18.5 1.4 copy.21
  20.0 29.9 %all-to-all-done.1 = bf16[128,4,1280]{0,2,1:T(8,128)(2,1)S(1)} async-done(((bf16[128,4,1280]{0,2,1:T(8,128)(2,1)}), bf16[128,4,1280]{0,2,1:T(8,128)(2,1)S(1)}, u32[]{:S(2)}, u32[]{:S(2)}) %all-to-all-start.1) | async-done | bytes 1310752 | tf_op jit(solution)/shard_map/all_to_all | solution.py:72
  49.9 4.3 %all-to-all-start = ((bf16[128,4,1280]{0,2,1:T(8,128)(2,1)}), bf16[128,4,1280]{0,2,1:T(8,128)(2,1)}, u32[]{:S(2)}, u32[]{:S(2)}) async-start(bf16[128,4,1280]{0,2,1:T(8,128)(2,1)} %bitcast), calls=%async_computation | async-start | bytes 2621440 | tf_op jit(solution)/shard_map/all_to_all | solution.py:73
  54.2 0.0 all-reduce.3.cloned.1.call-start
  54.2 0.0 copy-done.6
  54.2 0.6 fusion.15
  56.1 0.6 copy.24
  56.7 28.4 %all-to-all-done = bf16[128,4,1280]{0,2,1:T(8,128)(2,1)} async-done(((bf16[128,4,1280]{0,2,1:T(8,128)(2,1)}), bf16[128,4,1280]{0,2,1:T(8,128)(2,1)}, u32[]{:S(2)}, u32[]{:S(2)}) %all-to-all-start) | async-done | bytes 1310752 | tf_op jit(solution)/shard_map/all_to_all | solution.py:73
  85.1 1.6 copy.22
  86.7 2.8 broadcast_select_fusion.1
  89.4 0.0 all-reduce.3.cloned.1.call-update
  89.5 1.7 fusion.8
  91.1 0.0 copy-done.4
  91.1 0.0 copy-start.5
  91.1 0.0 copy-start.7
  91.2 2.8 fusion.10
  93.9 2.6 copy.28
  96.6 4.5 %all-to-all-start.2 = ((bf16[128,4,1280]{0,2,1:T(8,128)(2,1)}), bf16[128,4,1280]{0,2,1:T(8,128)(2,1)}, u32[]{:S(2)}, u32[]{:S(2)}) async-start(bf16[128,4,1280]{0,2,1:T(8,128)(2,1)} %bitcast.60), calls=%async_computation.2 | async-start | bytes 2621440 | tf_op jit(solution)/shard_map/all_to_all | solution.py:71
  101.1 0.0 copy-done.5
  101.1 0.1 reshape.102
  101.2 0.0 copy-done.7
  101.2 0.1 iota_compare_fusion
  101.3 80.3 %all-reduce.3.cloned.1.call-done = (bf16[2,512,1280]{2,1,0:T(8,128)(2,1)}, bf16[2,512,1280]{2,1,0:T(8,128)(2,1)}) async-done(((bf16[2,512,1280]{2,1,0:T(8,128)(2,1)}, bf16[2,512,1280]{2,1,0:T(8,128)(2,1)}), (bf16[2,512,1280]{2,1,0:T(8,128)(2,1)}, bf16[2,512,1280]{2,1,0:T(8,128)(2,1)})) %all-reduce.3.cloned.1.call-update) | async-done | bytes 5242896 | tf_op jit(solution)/shard_map/psum | solution.py:14
  181.5 4.4 %slice_bitcast_fusion.2 = (bf16[512,1280]{1,0:T(8,128)(2,1)}, bf16[512,1280]{1,0:T(8,128)(2,1)S(1)}, bf16[512,1280]{1,0:T(8,128)(2,1)S(1)}, bf16[512,1280]{1,0:T(8,128)(2,1)}) fusion(bf16[2,512,1280]{2,1,0:T(8,128)(2,1)} %get-tuple-element.19, bf16[2,512,1280]{2,1,0:T(8,128)(2,1)} %get-tuple-element.20), kind=kLoop, calls=%fused_computation.28 | loop fusion | bytes 10485760 | tf_op jit(solution)/shard_map/squeeze | solution.py:78
  185.9 2.1 pad_maximum_fusion.1
  188.0 8.6 %reshape.122 = bf16[12,128,10,128]{3,2,1,0:T(8,128)(2,1)} reshape(bf16[1536,1280]{1,0:T(8,128)(2,1)} %pad_maximum_fusion.1) | data formatting | bytes 7864320 | tf_op jit(solution)/shard_map/reshape | solution.py:30
  196.6 5.9 %copy.31 = bf16[12,128,10,128]{3,1,2,0:T(8,128)(2,1)} copy(bf16[12,128,10,128]{3,2,1,0:T(8,128)(2,1)} %reshape.122) | data formatting | bytes 7864320 | tf_op jit(solution)/shard_map/reshape | solution.py:30
  202.5 7.9 %gather_fusion.1 = bf16[32,128,10,128]{3,1,2,0:T(8,128)(2,1)} fusion(bf16[12,128,10,128]{3,1,2,0:T(8,128)(2,1)} %copy.31, s32[1024]{0:T(1024)S(1)} %pad_clamp_fusion), kind=kCustom, calls=%fused_computation.1 | custom fusion | bytes 20971648 | tf_op jit(solution)/shard_map/while/body/eval_jaxpr/gather | solution.py:42
  210.5 12.9 %copy.33 = bf16[4,8,128,10,128]{4,2,1,3,0:T(8,128)(2,1)} copy(bf16[4,8,128,10,128]{4,2,3,1,0:T(8,128)(2,1)} %bitcast.53) | data formatting | bytes 20971520 | tf_op jit(solution)/shard_map/while/body/eval_jaxpr/gather | solution.py:42
  223.3 0.0 copy-done.1
  223.3 3.3 %pad_maximum_fusion = bf16[1536,1280]{1,0:T(8,128)(2,1)} fusion(bf16[512,1280]{1,0:T(8,128)(2,1)S(1)} %copy-done.1, bf16[512,1280]{1,0:T(8,128)(2,1)} %get-tuple-element.42, bf16[512,1280]{1,0:T(8,128)(2,1)S(1)} %bitcast.57), kind=kLoop, calls=%fused_computation.10 | loop fusion | flops 11796480 | bytes 7864320 | tf_op jit(solution)/shard_map/concatenate | solution.py:31
  226.6 8.7 %reshape.121 = bf16[12,128,10,128]{3,2,1,0:T(8,128)(2,1)} reshape(bf16[1536,1280]{1,0:T(8,128)(2,1)} %pad_maximum_fusion) | data formatting | bytes 7864320 | tf_op jit(solution)/shard_map/reshape | solution.py:31
  235.3 5.8 %copy.27 = bf16[12,128,10,128]{3,1,2,0:T(8,128)(2,1)} copy(bf16[12,128,10,128]{3,2,1,0:T(8,128)(2,1)} %reshape.121) | data formatting | bytes 7864320 | tf_op jit(solution)/shard_map/reshape | solution.py:31
  241.1 8.0 %gather_fusion = bf16[32,128,10,128]{3,1,2,0:T(8,128)(2,1)} fusion(bf16[12,128,10,128]{3,1,2,0:T(8,128)(2,1)} %copy.27, s32[1024]{0:T(1024)S(1)} %pad_clamp_fusion), kind=kCustom, calls=%fused_computation | custom fusion | bytes 20971648 | tf_op jit(solution)/shard_map/while/body/eval_jaxpr/gather | solution.py:43
  249.1 0.0 all-to-all-done.2
  249.1 6.1 %fusion = (f32[4,10,128]{2,1,0:T(8,128)S(1)}, f32[4,10,128,1024]{2,3,1,0:S(1)}) fusion(pred[4,8]{1,0:T(4,128)(4,1)S(1)} %iota_compare_fusion, bf16[4,10,128,1024]{2,3,1,0:T(8,128)(2,1)} %bitcast.54, bf16[4,128,10,128]{1,3,2,0:T(8,128)(2,1)} %bitcast.16), kind=kOutput, calls=%fused_computation.5 | convolution fusion | flops 1357900800 | bytes 32788512
  255.2 4.9 %fusion.1 = f32[4,10,128]{2,1,0:T(8,128)S(1)} fusion(f32[4,10,128,1024]{2,3,1,0:S(1)} %get-tuple-element.40, f32[4,10,128]{2,1,0:T(8,128)S(1)} %get-tuple-element.39, pred[4,8]{1,0:T(4,128)(4,1)S(1)} %iota_compare_fusion), kind=kLoop, calls=%fused_computation.6 | loop fusion | flops 20966400 | bytes 21012512 | tf_op jit(solution)/shard_map/while/body/eval_jaxpr/reduce_sum | solution.py:54
  260.1 2.0 copy-done
  262.2 13.7 %bitcast_convert_fusion = bf16[4,10,128,128]{3,2,1,0:T(8,128)(2,1)S(1)} fusion(f32[4,10,128,1024]{2,3,1,0} %copy-done, f32[4,10,128]{2,1,0:T(8,128)S(1)} %fusion.1, f32[4,10,128]{2,1,0:T(8,128)S(1)} %get-tuple-element.39, pred[4,8]{1,0:T(4,128)(4,1)S(1)} %iota_compare_fusion, bf16[4,8,128,10,128]{4,2,3,1,0:T(8,128)(2,1)} %bitcast.55), kind=kOutput, calls=%fused_computation.23 | convolution fusion | flops 1369047040 | bytes 32808992 | tf_op jit(solution)/shard_map/while/body/eval_jaxpr/ghqkp,gkphd->gqhd/dot_general | solution.py:55
  275.8 35.7 %all_to_all.73 = bf16[4,128,1280]{1,2,0:T(8,128)(2,1)S(1)} all-to-all(bf16[4,128,1280]{1,2,0:T(8,128)(2,1)S(1)} %bitcast.63), channel_id=1, replica_groups=mesh['frame'=8,'head'=4] {'head'}, dimensions={0} | all-to-all | bytes 2621440 | tf_op jit(solution)/shard_map/all_to_all | solution.py:80
  311.6 1.4 copy.46
  (9 shorter events, 0.0 us)
Async XLA Ops:
  6.5 2.5 copy-start.3
  8.3 10.2 %copy-start.2 = (bf16[128,5120]{1,0:T(8,128)(2,1)S(1)}, bf16[128,5120]{1,0:T(8,128)(2,1)}, u32[]{:S(2)}) copy-start(bf16[128,5120]{1,0:T(8,128)(2,1)} %param.10) | copy-start | bytes 3932164
  12.1 42.2 %copy-start.6 = (s32[2]{0:T(128)S(1)}, s32[2]{0:T(128)}, u32[]{:S(2)}) copy-start(s32[2]{0:T(128)} %param.15) | copy-start | bytes 28
  12.1 37.8 %all-to-all-start.1 = ((bf16[128,4,1280]{0,2,1:T(8,128)(2,1)}), bf16[128,4,1280]{0,2,1:T(8,128)(2,1)S(1)}, u32[]{:S(2)}, u32[]{:S(2)}) async-start(bf16[128,4,1280]{0,2,1:T(8,128)(2,1)} %bitcast.4), calls=%async_computation.1 | async-start | bytes 2621440 | tf_op jit(solution)/shard_map/all_to_all | solution.py:72
  49.9 35.2 %all-to-all-start = ((bf16[128,4,1280]{0,2,1:T(8,128)(2,1)}), bf16[128,4,1280]{0,2,1:T(8,128)(2,1)}, u32[]{:S(2)}, u32[]{:S(2)}) async-start(bf16[128,4,1280]{0,2,1:T(8,128)(2,1)} %bitcast), calls=%async_computation | async-start | bytes 2621440 | tf_op jit(solution)/shard_map/all_to_all | solution.py:73
  54.2 127.4 %all-reduce.3.cloned.1.call-start = ((), (), s32[]{:S(2)}) async-start(), calls=%async_computation.4 | async-start | bytes 10485760 | tf_op jit(solution)/shard_map/psum | solution.py:14
  89.4 1.7 copy-start.4
  91.1 9.9 %copy-start.5 = (s32[1,4,8]{2,1,0:T(4,128)S(1)}, s32[1,4,8]{2,1,0:T(4,128)}, u32[]{:S(2)}) copy-start(s32[1,4,8]{2,1,0:T(4,128)} %param.13) | copy-start | bytes 388
  91.1 10.0 %copy-start.7 = (s32[1,4]{1,0:T(1,128)S(1)}, s32[1,4]{1,0:T(1,128)}, u32[]{:S(2)}) copy-start(s32[1,4]{1,0:T(1,128)} %param.14) | copy-start | bytes 52
  96.6 152.5 %all-to-all-start.2 = ((bf16[128,4,1280]{0,2,1:T(8,128)(2,1)}), bf16[128,4,1280]{0,2,1:T(8,128)(2,1)}, u32[]{:S(2)}, u32[]{:S(2)}) async-start(bf16[128,4,1280]{0,2,1:T(8,128)(2,1)} %bitcast.60), calls=%async_computation.2 | async-start | bytes 2621440 | tf_op jit(solution)/shard_map/all_to_all | solution.py:71
  210.4 12.9 %copy-start.1 = (bf16[512,1280]{1,0:T(8,128)(2,1)S(1)}, bf16[512,1280]{1,0:T(8,128)(2,1)}, u32[]{:S(2)}) copy-start(bf16[512,1280]{1,0:T(8,128)(2,1)} %get-tuple-element.23) | copy-start | bytes 3932164
  255.2 7.0 %copy-start = (f32[4,10,128,1024]{2,3,1,0}, f32[4,10,128,1024]{2,3,1,0:S(1)}, u32[]{:S(2)}) copy-start(f32[4,10,128,1024]{2,3,1,0:S(1)} %get-tuple-element.40) | copy-start | bytes 62914564
Sparse Core Ops, SparseCore 0:
  89.6 91.8 all-reduce.2
where the time goes:
time: 321 us; the launch traced here: 320 us
  waiting for transfers between devices  139 us (43%)
  local copies, waits for them, and re-layouts  74.4 us (23%)
  blocking collectives  35.7 us (11%)
  other arithmetic  21.3 us (7%)
  matrix products  19.8 us (6%)
  starting transfers between devices  15.3 us (5%)
  between operations  14.8 us (5%)
    psum x1, waiting for transfers between devices, spread(): return lax.psum(block, axis)  80.3 us
    all_to_all x1, blocking collectives, shards(): lax.all_to_all(mixed, 'head', split_axis=0, concat_axis=1, tiled=True)  35.7 us
    all_to_all x1, waiting for transfers between devices, shards(): lax.all_to_all(k_norm, 'head', split_axis=1, concat_axis=0, tiled=True)  29.9 us
    all_to_all x1, waiting for transfers between devices, shards(): lax.all_to_all(values, 'head', split_axis=1, concat_axis=0, tiled=True)  28.4 us
    gather x2, local copies, waits for them, and re-layouts, one_group(): picked_k = key_blocks[id_lists]  20.8 us
    reshape x2, local copies, waits for them, and re-layouts, attend_view(): jnp.concatenate([k_heads] + far_keys, axis=0)  14.5 us
    reshape x2, local copies, waits for them, and re-layouts, attend_view(): jnp.concatenate([v_heads] + far_values, axis=0)  14.5 us
    dot_general x1, matrix products, one_group(): jnp.einsum('ghqkp,gkphd->gqhd', weights, picked_v, preferred_element_type...  13.7 us
  transfers between devices with their start and end apart: 4, of which 3 were waited for; matrix products, arithmetic and copies ran while one was open for 24% of the time, Pallas kernels for 0%

commit v1 on v0

v1 whole, which is shorter than its diff:
```python
import functools
import math

import jax
import jax.numpy as jnp
from jax import lax
from jax.experimental import pallas as pl
from jax.experimental.pallas import tpu as pltpu
from jax.sharding import PartitionSpec as P

HD = 128
BLOCK = 128
WINDOW = 3
EPS = 1e-06
MESH = pl.DeviceIdType.MESH


def columns(head):
    return pl.ds(pl.multiple_of(head * HD, HD), HD)


def kernel(
    nz, nf, bits, heads, anchor_total, listed,
    ids_ref, counts_ref, anchors_ref, q_ref, k_ref, v_ref, qg_ref, kg_ref, out_ref,
    qn, kn, kv, qb, core_in, hop_out, hop_in, mixed, bias,
    in_send, in_recv, core_send, core_recv, hop_send, hop_recv, pair_send, pair_recv, out_send, out_recv,
):
    f = lax.axis_index("frame")
    z = lax.axis_index("head")
    all_heads = nz * heads
    total = nz * (1 + anchor_total)
    hops = bits - 1
    me_bits = [lax.rem(lax.div(f, 2**k), 2) for k in range(bits)]
    partners = [f + (2**k) * (1 - 2 * me_bits[k]) for k in range(bits)]
    core = me_bits[0]

    barrier = pltpu.get_barrier_semaphore()
    for d in range(1, nz):
        pl.semaphore_signal(barrier, inc=1, device_id={"head": lax.rem(z + d, nz)}, device_id_type=MESH)
    for k in range(bits):
        pl.semaphore_signal(barrier, inc=1, device_id={"frame": partners[k]}, device_id_type=MESH)

    def in_copy(kind, j, d):
        to = lax.rem(z + d, nz)
        head = to * heads + j
        if kind == 0:
            src, dst = kn.at[head], kv.at[0, j, z]
        elif kind == 1:
            src, dst = v_ref.at[:, columns(head)], kv.at[1, j, z]
        else:
            src, dst = qn.at[head], qb.at[j, z]
        return pltpu.make_async_remote_copy(
            src_ref=src, dst_ref=dst, send_sem=in_send.at[kind, j, d], recv_sem=in_recv.at[kind, j, d],
            device_id={"head": to}, device_id_type=MESH,
        )

    def out_copy(j, d):
        to = lax.rem(z + d, nz)
        return pltpu.make_async_remote_copy(
            src_ref=mixed.at[j, to], dst_ref=out_ref.at[:, columns(z * heads + j)],
            send_sem=out_send.at[j, d], recv_sem=out_recv.at[j, d],
            device_id={"head": to}, device_id_type=MESH,
        )

    def core_copy(j):
        return pltpu.make_async_remote_copy(
            src_ref=kv.at[1 - core, j, pl.ds(0, nz)], dst_ref=core_in.at[j],
            send_sem=core_send.at[j], recv_sem=core_recv.at[j],
            device_id={"frame": partners[0]}, device_id_type=MESH,
        )

    def hop_copy(k, j):
        return pltpu.make_async_remote_copy(
            src_ref=hop_out.at[k, j], dst_ref=hop_in.at[k, j],
            send_sem=hop_send.at[k, j], recv_sem=hop_recv.at[k, j],
            device_id={"frame": partners[k + 1]}, device_id_type=MESH,
        )

    def pair_copy(j):
        far = kv.at[core, j, pl.ds(nz, nz * anchor_total)]
        return pltpu.make_async_remote_copy(
            src_ref=far, dst_ref=far, send_sem=pair_send.at[j], recv_sem=pair_recv.at[j],
            device_id={"frame": partners[0]}, device_id_type=MESH,
        )

    def kinds_of(unit, act):
        @pl.when(unit < heads)
        def _():
            for kind in (0, 1):
                for d in range(1, nz):
                    act(in_copy(kind, unit, d))

        @pl.when(unit >= heads)
        def _():
            for d in range(1, nz):
                act(in_copy(2, unit - heads, d))

    def send_unit(unit):
        kinds_of(unit, lambda copy: copy.start())

    def unit_sent(unit):
        kinds_of(unit, lambda copy: copy.wait_send())

    def normalize(src, gain, dst):
        def square(h, acc):
            wide = src[:, columns(h)].astype(jnp.float32)
            return acc + wide * wide

        acc = lax.fori_loop(0, all_heads, square, jnp.zeros((BLOCK, HD), jnp.float32))
        mean = jnp.sum(acc, axis=1, keepdims=True) * (1.0 / (all_heads * HD))
        factor = lax.rsqrt(mean + EPS)

        def write(h, carry):
            wide = src[:, columns(h)].astype(jnp.float32)
            dst[h] = (wide * factor * gain[:, columns(h)]).astype(jnp.bfloat16)
            return carry

        lax.fori_loop(0, all_heads, write, 0)

    normalize(k_ref, kg_ref, kn)
    pl.semaphore_wait(barrier, nz - 1 + bits)
    for unit in range(WINDOW):
        send_unit(jnp.int32(unit))
    normalize(q_ref, qg_ref, qn)

    def own(j, carry):
        head = z * heads + j
        kv[0, j, z] = kn[head]
        kv[1, j, z] = v_ref[:, columns(head)]
        qb[j, z] = qn[head]
        return carry

    lax.fori_loop(0, heads, own, 0)

    for b in range(nz):
        count = counts_ref[0, b]
        wanted = [lax.select(count > s, ids_ref[0, b, s], jnp.int32(-1)) for s in range(listed)]
        for c in range(total):
            hit = wanted[0] == c
            for s in range(1, listed):
                hit = jnp.logical_or(hit, wanted[s] == c)
            value = lax.select(hit, jnp.float32(0.0), jnp.float32(-1e30))
            bias[b, :, c * BLOCK:(c + 1) * BLOCK] = jnp.full((8, BLOCK), value, jnp.float32)

    def mine(a, k):
        bit = lax.rem(lax.div(anchors_ref[a], jnp.int32(2**k)), jnp.int32(2))
        return bit == me_bits[k]

    flags = [[mine(a, k) for k in range(bits)] for a in range(anchor_total)]
    scale = 1.0 / math.sqrt(HD)
    first = max(heads, 2 * hops)

    def step(t, carry):
        @pl.when(t + WINDOW < 2 * heads)
        def _():
            @pl.when(t < heads)
            def _():
                for kind in (0, 1):
                    for d in range(1, nz):
                        in_copy(kind, t, d).wait_recv()

            send_unit(t + WINDOW)

        @pl.when(jnp.logical_and(t < heads, t + WINDOW >= 2 * heads))
        def _():
            for kind in (0, 1):
                for d in range(1, nz):
                    in_copy(kind, t, d).wait_recv()

        @pl.when(t < heads)
        def _():
            core_copy(t).start()

        for k in reversed(range(hops)):
            j = t - 2 * (k + 1)

            @pl.when(jnp.logical_and(j >= 0, j < heads))
            def _():
                hop_copy(k, j).wait_recv()
                for a in range(anchor_total):
                    for n in range(nz):
                        picked = lax.select_n(flags[a][k + 1], hop_in[k, j, a, n], hop_out[k, j, a, n])
                        if k == hops - 1:
                            kv[core, j, nz * (1 + a) + n] = picked
                        else:
                            hop_out[k + 1, j, a, n] = picked
                if k == hops - 1:
                    pair_copy(j).start()
                else:
                    hop_copy(k + 1, j).start()

        @pl.when(t < heads)
        def _():
            core_copy(t).wait_recv()
            for a in range(anchor_total):
                for n in range(nz):
                    hop_out[0, t, a, n] = lax.select_n(flags[a][0], core_in[t, n], kv[core, t, n])
            hop_copy(0, t).start()

        @pl.when(t >= first)
        def _():
            e = t - first
            for d in range(1, nz):
                in_copy(2, e, d).wait_recv()
            pair_copy(e).wait_recv()

            def attend(b, inner):
                k_all = kv[0, e].reshape(total * BLOCK, HD)
                v_all = kv[1, e].reshape(total * BLOCK, HD)
                scores = lax.dot_general(
                    qb[e, b], k_all, (((1,), (1,)), ((), ())), preferred_element_type=jnp.float32
                )
                scores = scores * scale + bias[b, 0:1, :]
                top = jnp.max(scores, axis=1, keepdims=True)
                expo = jnp.exp(scores - top)
                weights = (expo * (1.0 / jnp.sum(expo, axis=1, keepdims=True))).astype(jnp.bfloat16)
                mixed[e, b] = jnp.dot(weights, v_all, preferred_element_type=jnp.float32).astype(jnp.bfloat16)
                return inner

            lax.fori_loop(0, nz, attend, 0)
            for d in range(1, nz):
                out_copy(e, d).start()
            out_ref[:, columns(z * heads + e)] = mixed[e, z]
            unit_sent(2 * e)
            unit_sent(2 * e + 1)
            core_copy(e).wait_send()
            for k in range(hops):
                hop_copy(k, e).wait_send()
            pair_copy(e).wait_send()

            @pl.when(e >= 2)
            def _():
                for d in range(1, nz):
                    out_copy(e - 2, d).wait_send()

        return carry

    lax.fori_loop(0, first + heads, step, 0)

    for e in range(max(heads - 2, 0), heads):
        for d in range(1, nz):
            out_copy(e, d).wait_send()

    def arrived(e, carry):
        for d in range(1, nz):
            out_copy(e, d).wait_recv()
        return carry

    lax.fori_loop(0, heads, arrived, 0)


def shards(nz, nf, queries, keys, values, q_gain, k_gain, block_ids, counts, anchors):
    rows, width = queries.shape
    bits = nf.bit_length() - 1
    hops = bits - 1
    all_heads = width // HD
    heads = all_heads // nz
    anchor_total = anchors.shape[0]
    total = nz * (1 + anchor_total)
    listed = block_ids.shape[2]
    tile = (BLOCK, HD)
    bf = jnp.bfloat16
    dma = pltpu.SemaphoreType.DMA
    smem = pl.BlockSpec(memory_space=pltpu.SMEM)
    vmem = pl.BlockSpec(memory_space=pltpu.VMEM)
    return pl.pallas_call(
        functools.partial(kernel, nz, nf, bits, heads, anchor_total, listed),
        out_shape=jax.ShapeDtypeStruct((rows, width), bf),
        in_specs=[smem] * 3 + [vmem] * 5,
        out_specs=vmem,
        scratch_shapes=[
            pltpu.VMEM((all_heads,) + tile, bf),
            pltpu.VMEM((all_heads,) + tile, bf),
            pltpu.VMEM((2, heads, total) + tile, bf),
            pltpu.VMEM((heads, nz) + tile, bf),
            pltpu.VMEM((heads, nz) + tile, bf),
            pltpu.VMEM((hops, heads, anchor_total, nz) + tile, bf),
            pltpu.VMEM((hops, heads, anchor_total, nz) + tile, bf),
            pltpu.VMEM((heads, nz) + tile, bf),
            pltpu.VMEM((nz, 8, total * BLOCK), jnp.float32),
            dma((3, heads, nz)),
            dma((3, heads, nz)),
            dma((heads,)),
            dma((heads,)),
            dma((hops, heads)),
            dma((hops, heads)),
            dma((heads,)),
            dma((heads,)),
            dma((heads, nz)),
            dma((heads, nz)),
        ],
        compiler_params=pltpu.CompilerParams(
            collective_id=0, has_side_effects=True, vmem_limit_bytes=56 * 1024 * 1024
        ),
    )(block_ids, counts, anchors, queries, keys, values, q_gain[None, :], k_gain[None, :])


def solution(mesh):
    placed = (
        P(("frame", "head"), None),
        P(("frame", "head"), None),
        P(("frame", "head"), None),
        P(),
        P(),
        P("frame", None, None),
        P("frame", None),
        P(),
    )
    return jax.shard_map(
        functools.partial(shards, mesh.shape["head"], mesh.shape["frame"]),
        mesh=mesh, in_specs=placed, out_specs=P(("frame", "head"), None), check_vma=False,
    )
```

time: 321 us -> 135 us (0.42)
  waiting for transfers between devices: 139 us -> 0 us
  Pallas kernels: 0 us -> 133 us
  local copies, waits for them, and re-layouts: 74.4 us -> 2.46 us
  blocking collectives: 35.7 us -> 0 us
  other arithmetic: 21.3 us -> 0 us
  matrix products: 19.8 us -> 0 us
  starting transfers between devices: 15.3 us -> 0 us
  between operations: 14.8 us -> 0.01 us
    pallas_call x0 -> x1, Pallas kernels: none -> 133 us  [shards(): pl.pallas_call(functools.partial(kernel, nz, nf, bits, heads, anchor_tota...]
    psum x1 -> x0, waiting for transfers between devices: 80.3 us -> none  [spread(): return lax.psum(block, axis)]
    all_to_all x3 -> x0, waiting for transfers between devices: 58.3 us -> none  [the longest x1 29.9 us: shards(): lax.all_to_all(k_norm, 'head', split_axis=1, concat_axis=0, tiled=True)]
    all_to_all x1 -> x0, blocking collectives: 35.7 us -> none  [shards(): lax.all_to_all(mixed, 'head', split_axis=0, concat_axis=1, tiled=True)]
    reshape x4 -> x0, local copies, waits for them, and re-layouts: 29 us -> none  [the longest x2 14.5 us: attend_view(): jnp.concatenate([k_heads] + far_keys, axis=0)]
    gather x3 -> x0, local copies, waits for them, and re-layouts: 28.9 us -> none  [the longest x2 20.8 us: one_group(): picked_k = key_blocks[id_lists]]
    all_to_all x3 -> x0, starting transfers between devices: 15.2 us -> none  [the longest x1 6.45 us: shards(): lax.all_to_all(k_norm, 'head', split_axis=1, concat_axis=0, tiled=True)]
    dot_general x1 -> x0, matrix products: 13.7 us -> none  [one_group(): jnp.einsum('ghqkp,gkphd->gqhd', weights, picked_v, preferred_element_type...]
  transfers between devices with their start and end apart: 4 -> 0, of which waited for: 3 -> 0; matrix products, arithmetic and copies ran while one was open for 24% -> 0% of each run, Pallas kernels for 0% -> 0%
where the time goes in v1:
time: 135 us
  Pallas kernels  133 us (99%)
  local copies, waits for them, and re-layouts  2.46 us (2%)
    pallas_call x1, Pallas kernels, shards(): pl.pallas_call(functools.partial(kernel, nz, nf, bits, heads, anchor_tota...  133 us

profile of v1, /device:TPU:0, one launch (start us, length us, event | category | flops | bytes accessed | tf_op | source)
XLA Modules:
  0.0 135.3 jit_solution(16676771205553062293)
XLA Ops:
  0.0 132.8 %shard_map.82 = bf16[128,5120]{1,0:T(8,128)(2,1)} custom-call(s32[1,4,8]{2,1,0:T(4,128)} %ids_ref.1, s32[1,4]{1,0:T(1,128)} %counts_ref.1, s32[2]{0:T(128)} %anchors_ref.1, bf16[128,5120]{1,0:T(8,128)(2,1)} %q_ref.1, bf16[128,5120]{1,0:T(8,128)(2,1)} %k_ref.1, bf16[128,5120]{1,0:T(8,128)(2,1)} %v_ref.1, f32[1,5120]{1,0:T(1,128)} %bitcast.2, f32[1,5120]{1,0:T(1,128)} %bitcast.3), custom_call_target="tpu_custom_call" | custom-call | tf_op jit(solution)/shard_map/pallas_call | solution.py:266
  132.9 2.5 %copy.10 = bf16[128,5120]{1,0:T(8,128)(2,1)} copy(bf16[128,5120]{1,0:T(8,128)(2,1)} %shard_map.82) | data formatting | bytes 2621440

commit v2 on v1

--- a/solution.py
+++ b/solution.py
@@ -21,8 +21,8 @@
 
 def kernel(
     nz, nf, bits, heads, anchor_total, listed,
-    ids_ref, counts_ref, anchors_ref, q_ref, k_ref, v_ref, qg_ref, kg_ref, out_ref,
-    qn, kn, kv, qb, core_in, hop_out, hop_in, mixed, bias,
+    ids_ref, counts_ref, anchors_ref, q_hbm, k_hbm, v_hbm, qg_ref, kg_ref, out_ref,
+    q_ref, k_ref, v_ref, load_sem, qn, kn, kv, qb, core_in, hop_out, hop_in, mixed, bias,
     in_send, in_recv, core_send, core_recv, hop_send, hop_recv, pair_send, pair_recv, out_send, out_recv,
 ):
     f = lax.axis_index("frame")
@@ -34,6 +34,12 @@
     partners = [f + (2**k) * (1 - 2 * me_bits[k]) for k in range(bits)]
     core = me_bits[0]
 
+    loads = [
+        pltpu.make_async_copy(src, dst, load_sem.at[n])
+        for n, (src, dst) in enumerate(((v_hbm, v_ref), (k_hbm, k_ref), (q_hbm, q_ref)))
+    ]
+    for load in loads:
+        load.start()
     barrier = pltpu.get_barrier_semaphore()
     for d in range(1, nz):
         pl.semaphore_signal(barrier, inc=1, device_id={"head": lax.rem(z + d, nz)}, device_id_type=MESH)
@@ -86,7 +92,7 @@
     def kinds_of(unit, act):
         @pl.when(unit < heads)
         def _():
-            for kind in (0, 1):
+            for kind in (1, 0):
                 for d in range(1, nz):
                     act(in_copy(kind, unit, d))
 
@@ -117,10 +123,17 @@
 
         lax.fori_loop(0, all_heads, write, 0)
 
-    normalize(k_ref, kg_ref, kn)
+    loads[0].wait()
     pl.semaphore_wait(barrier, nz - 1 + bits)
     for unit in range(WINDOW):
-        send_unit(jnp.int32(unit))
+        for d in range(1, nz):
+            in_copy(1, unit, d).start()
+    loads[1].wait()
+    normalize(k_ref, kg_ref, kn)
+    for unit in range(WINDOW):
+        for d in range(1, nz):
+            in_copy(0, unit, d).start()
+    loads[2].wait()
     normalize(q_ref, qg_ref, qn)
 
     def own(j, carry):
@@ -147,7 +160,7 @@
         return bit == me_bits[k]
 
     flags = [[mine(a, k) for k in range(bits)] for a in range(anchor_total)]
-    scale = 1.0 / math.sqrt(HD)
+    scale = math.log2(math.e) / math.sqrt(HD)
     first = max(heads, 2 * hops)
 
     def step(t, carry):
@@ -204,7 +217,8 @@
                 in_copy(2, e, d).wait_recv()
             pair_copy(e).wait_recv()
 
-            def attend(b, inner):
+            def attend(i, inner):
+                b = lax.rem(z + 1 + i, nz)
                 k_all = kv[0, e].reshape(total * BLOCK, HD)
                 v_all = kv[1, e].reshape(total * BLOCK, HD)
                 scores = lax.dot_general(
@@ -212,14 +226,17 @@
                 )
                 scores = scores * scale + bias[b, 0:1, :]
                 top = jnp.max(scores, axis=1, keepdims=True)
-                expo = jnp.exp(scores - top)
+                expo = jnp.exp2(scores - top)
                 weights = (expo * (1.0 / jnp.sum(expo, axis=1, keepdims=True))).astype(jnp.bfloat16)
                 mixed[e, b] = jnp.dot(weights, v_all, preferred_element_type=jnp.float32).astype(jnp.bfloat16)
+
+                @pl.when(i < nz - 1)
+                def _():
+                    out_copy(e, i + 1).start()
+
                 return inner
 
             lax.fori_loop(0, nz, attend, 0)
-            for d in range(1, nz):
-                out_copy(e, d).start()
             out_ref[:, columns(z * heads + e)] = mixed[e, z]
             unit_sent(2 * e)
             unit_sent(2 * e + 1)
@@ -266,9 +283,13 @@
     return pl.pallas_call(
         functools.partial(kernel, nz, nf, bits, heads, anchor_total, listed),
         out_shape=jax.ShapeDtypeStruct((rows, width), bf),
-        in_specs=[smem] * 3 + [vmem] * 5,
+        in_specs=[smem] * 3 + [pl.BlockSpec(memory_space=pl.ANY)] * 3 + [vmem] * 2,
         out_specs=vmem,
         scratch_shapes=[
+            pltpu.VMEM((rows, width), bf),
+            pltpu.VMEM((rows, width), bf),
+            pltpu.VMEM((rows, width), bf),
+            dma((3,)),
             pltpu.VMEM((all_heads,) + tile, bf),
             pltpu.VMEM((all_heads,) + tile, bf),
             pltpu.VMEM((2, heads, total) + tile, bf),

time: 135 us -> 131 us (0.970)
  Pallas kernels: 133 us -> 129 us
    pallas_call x1, Pallas kernels: 133 us -> 129 us  [shards(): pl.pallas_call(functools.partial(kernel, nz, nf, bits, heads, anchor_tota...]
where the time goes in v2:
time: 131 us
  Pallas kernels  129 us (98%)
  local copies, waits for them, and re-layouts  2.46 us (2%)
    pallas_call x1, Pallas kernels, shards(): pl.pallas_call(functools.partial(kernel, nz, nf, bits, heads, anchor_tota...  129 us

profile of v2, /device:TPU:0, one launch (start us, length us, event | category | flops | bytes accessed | tf_op | source)
XLA Modules:
  0.0 131.3 jit_solution(5375366261144179535)
XLA Ops:
  0.0 128.8 %shard_map.82 = bf16[128,5120]{1,0:T(8,128)(2,1)} custom-call(s32[1,4,8]{2,1,0:T(4,128)} %ids_ref.1, s32[1,4]{1,0:T(1,128)} %counts_ref.1, s32[2]{0:T(128)} %anchors_ref.1, bf16[128,5120]{1,0:T(8,128)(2,1)} %q_hbm.1, bf16[128,5120]{1,0:T(8,128)(2,1)} %k_hbm.1, bf16[128,5120]{1,0:T(8,128)(2,1)} %v_hbm.1, f32[1,5120]{1,0:T(1,128)} %bitcast.2, f32[1,5120]{1,0:T(1,128)} %bitcast.3), custom_call_target="tpu_custom_call" | custom-call | tf_op jit(solution)/shard_map/pallas_call | solution.py:283
  128.8 2.5 %copy.10 = bf16[128,5120]{1,0:T(8,128)(2,1)} copy(bf16[128,5120]{1,0:T(8,128)(2,1)} %shard_map.82) | data formatting | bytes 2621440

commit v3 on v2

--- a/solution.py
+++ b/solution.py
@@ -10,7 +10,7 @@
 
 HD = 128
 BLOCK = 128
-WINDOW = 3
+WINDOW = 5
 EPS = 1e-06
 MESH = pl.DeviceIdType.MESH
 
@@ -33,6 +33,7 @@
     me_bits = [lax.rem(lax.div(f, 2**k), 2) for k in range(bits)]
     partners = [f + (2**k) * (1 - 2 * me_bits[k]) for k in range(bits)]
     core = me_bits[0]
+    window = min(WINDOW, heads)
 
     loads = [
         pltpu.make_async_copy(src, dst, load_sem.at[n])
@@ -125,12 +126,12 @@
 
     loads[0].wait()
     pl.semaphore_wait(barrier, nz - 1 + bits)
-    for unit in range(WINDOW):
+    for unit in range(window):
         for d in range(1, nz):
             in_copy(1, unit, d).start()
     loads[1].wait()
     normalize(k_ref, kg_ref, kn)
-    for unit in range(WINDOW):
+    for unit in range(window):
         for d in range(1, nz):
             in_copy(0, unit, d).start()
     loads[2].wait()
@@ -164,7 +165,7 @@
     first = max(heads, 2 * hops)
 
     def step(t, carry):
-        @pl.when(t + WINDOW < 2 * heads)
+        @pl.when(t + window < 2 * heads)
         def _():
             @pl.when(t < heads)
             def _():
@@ -172,9 +173,9 @@
                     for d in range(1, nz):
                         in_copy(kind, t, d).wait_recv()
 
-            send_unit(t + WINDOW)
-
-        @pl.when(jnp.logical_and(t < heads, t + WINDOW >= 2 * heads))
+            send_unit(t + window)
+
+        @pl.when(jnp.logical_and(t < heads, t + window >= 2 * heads))
         def _():
             for kind in (0, 1):
                 for d in range(1, nz):

time: 131 us -> 135 us (1.031)
  Pallas kernels: 129 us -> 132 us
    pallas_call x1, Pallas kernels: 129 us -> 132 us  [shards(): pl.pallas_call(functools.partial(kernel, nz, nf, bits, heads, anchor_tota...]
where the time goes in v3:
time: 135 us
  Pallas kernels  132 us (98%)
  local copies, waits for them, and re-layouts  2.46 us (2%)
    pallas_call x1, Pallas kernels, shards(): pl.pallas_call(functools.partial(kernel, nz, nf, bits, heads, anchor_tota...  132 us

profile of v3, /device:TPU:0, one launch (start us, length us, event | category | flops | bytes accessed | tf_op | source)
XLA Modules:
  0.0 134.7 jit_solution(1133678698160995659)
XLA Ops:
  0.0 132.3 %shard_map.82 = bf16[128,5120]{1,0:T(8,128)(2,1)} custom-call(s32[1,4,8]{2,1,0:T(4,128)} %ids_ref.1, s32[1,4]{1,0:T(1,128)} %counts_ref.1, s32[2]{0:T(128)} %anchors_ref.1, bf16[128,5120]{1,0:T(8,128)(2,1)} %q_hbm.1, bf16[128,5120]{1,0:T(8,128)(2,1)} %k_hbm.1, bf16[128,5120]{1,0:T(8,128)(2,1)} %v_hbm.1, f32[1,5120]{1,0:T(1,128)} %bitcast.2, f32[1,5120]{1,0:T(1,128)} %bitcast.3), custom_call_target="tpu_custom_call" | custom-call | tf_op jit(solution)/shard_map/pallas_call | solution.py:284
  132.3 2.5 %copy.10 = bf16[128,5120]{1,0:T(8,128)(2,1)} copy(bf16[128,5120]{1,0:T(8,128)(2,1)} %shard_map.82) | data formatting | bytes 2621440
